TPU v7x, 256 devices: a whole 4x4x8 slice. The times are simulated.
256 devices in a mesh: seq: 64 (over y, z, core), chan: 4 (over x).
Axes of the slice: x: 4, y: 4, z: 8, core: 2. Of those that a mesh axis runs over, the one named last changes fastest.
Arguments:
- inputs: bfloat16 [32768, 1536], P('seq', 'chan'), may hold values from -16 to 16
- conv_weight: bfloat16 [1, 3, 1536, 1536], P(None, None, None, 'chan'), may hold values from -0.09375 to 0.09375
- head_weight: bfloat16 [1536, 4096], P(None, 'chan'), may hold values from -0.15625 to 0.15625
- head_cot: bfloat16 [32768, 4096], P('seq', 'chan'), may hold values from -6 to 6
- exon_blocks: int32 [512, 8], P('seq'), may hold values from 0 to 255
Outputs:
- tracks: bfloat16 [32768, 4096], P('seq', 'chan')
- coverage: float32 [512, 4096], P('seq', 'chan')
- input_grad: bfloat16 [32768, 1536], P('seq', 'chan')
- kernel_gradient: float32 [1, 3, 1536, 1536], P(None, None, 'seq', 'chan')
All inputs are finite; a program needn't handle non-finite values.
Results may differ from a plain program's by a relative error of at most 0.0059.
Values may be sent and summed in bfloat16 or wider, within the bound.
No kernel may reach another device: no remote copies, remote signals or barrier semaphores. Data moves between devices by JAX's collectives and lax.ppermute only.
A program may use at most 64 MiB of HBM per device.

v0:
```python
import jax
import jax.numpy as jnp
from jax import lax
from jax.sharding import PartitionSpec as P

BLOCK = 128
EXONS = 8


def shifted(value, axis, steps):
    count = lax.axis_size(axis)
    leading, last = (max(0, -steps), min(count, count - steps))
    return lax.ppermute(value, axis, [(source, source + steps) for source in range(leading, last)])


def activation_slope(point, cotan):
    _, back = jax.vjp(jax.nn.gelu, point)
    return back(cotan)[0]


def tap_input(values, steps):
    return shifted(values, "seq", steps)


def tap_grad(values, steps):
    return shifted(values, "seq", steps)


def times_t(left, right):
    return lax.dot_general(
        left, right, (((1,), (1,)), ((), ())), preferred_element_type=jnp.float32
    )


def inner_rows(left, right):
    return lax.dot_general(
        left, right, (((0,), (0,)), ((), ())), preferred_element_type=jnp.float32
    )


def shards(inputs, conv_weight, head_weight, head_cot, exon_blocks):
    rows = inputs.shape[0]
    state = inputs
    layer_number = 0
    steps = 2 * 2**layer_number
    acted = jax.nn.gelu(state.astype(jnp.float32)).astype(jnp.bfloat16)
    lower = tap_input(acted, steps)
    upper = tap_input(acted, -steps)
    whole = lax.all_gather(acted, "chan", axis=1, tiled=True)
    whole_low = lax.all_gather(lower, "chan", axis=1, tiled=True)
    whole_up = lax.all_gather(upper, "chan", axis=1, tiled=True)
    mixed = jnp.dot(whole_low, conv_weight[layer_number, 0], preferred_element_type=jnp.float32)
    mixed = mixed + jnp.dot(whole, conv_weight[layer_number, 1], preferred_element_type=jnp.float32)
    mixed = mixed + jnp.dot(
        whole_up, conv_weight[layer_number, 2], preferred_element_type=jnp.float32
    )
    saved = [(state, whole, steps)]
    state = (state.astype(jnp.float32) + mixed).astype(jnp.bfloat16)
    full_state = lax.all_gather(state, "chan", axis=1, tiled=True)
    logits = jnp.dot(full_state, head_weight, preferred_element_type=jnp.float32)
    tracks = jax.nn.softplus(logits).astype(jnp.bfloat16)
    head_term = (head_cot.astype(jnp.float32) * jax.nn.sigmoid(logits)).astype(jnp.bfloat16)
    grad = lax.psum_scatter(
        times_t(head_term, head_weight), "chan", scatter_dimension=1, tiled=True
    )
    grads = []
    for layer_number in reversed(range(conv_weight.shape[0])):
        before, whole, steps = saved[layer_number]
        grad_low = grad.astype(jnp.bfloat16)
        later = tap_grad(grad_low, -steps)
        earlier = tap_grad(grad_low, steps)
        partial_value = times_t(later, conv_weight[layer_number, 0])
        partial_value = partial_value + times_t(grad_low, conv_weight[layer_number, 1])
        partial_value = partial_value + times_t(earlier, conv_weight[layer_number, 2])
        back_u = lax.psum_scatter(partial_value, "chan", scatter_dimension=1, tiled=True)
        kernel = jnp.stack(
            [inner_rows(whole, later), inner_rows(whole, grad_low), inner_rows(whole, earlier)]
        )
        grads.append(lax.psum_scatter(kernel, "seq", scatter_dimension=1, tiled=True))
        grad = grad + activation_slope(before.astype(jnp.float32), back_u)
    kernel_gradient = jnp.stack(grads[::-1])
    resident_blocks = rows // BLOCK
    block_partial_sums = (
        tracks.astype(jnp.float32).reshape(resident_blocks, BLOCK, tracks.shape[1]).sum(axis=1)
    )
    scale = jnp.sqrt(jnp.float32(EXONS * BLOCK))
    all_blocks = lax.all_gather(block_partial_sums, "seq", axis=0, tiled=True)
    labels = jnp.arange(all_blocks.shape[0], dtype=jnp.int32)
    counts = jnp.sum((exon_blocks[:, :, None] == labels[None, None, :]).astype(jnp.float32), axis=1)
    coverage = jnp.dot(counts, all_blocks, precision=lax.Precision.HIGHEST) / scale
    return (tracks, coverage, grad.astype(jnp.bfloat16), kernel_gradient)


def solution(mesh):
    return jax.shard_map(
        shards,
        mesh=mesh,
        in_specs=(
            P("seq", "chan"),
            P(None, None, None, "chan"),
            P(None, "chan"),
            P("seq", "chan"),
            P("seq", None),
        ),
        out_specs=(
            P("seq", "chan"),
            P("seq", "chan"),
            P("seq", "chan"),
            P(None, None, "seq", "chan"),
        ),
        check_vma=False,
    )
```

profile of v0, /device:TPU:2, one launch (start us, length us, event | category | flops | bytes accessed | tf_op | source)
XLA Modules:
  0.0 468.9 jit_solution(14514463337364591084)
XLA Ops:
  7.2 0.0 all-gather.9.cloned.1.call-start
  7.2 2.2 fusion.30
  9.4 0.0 all-gather.9.cloned.1.call-update
  9.4 0.0 all-gather.11.cloned.1.call-start
  9.5 1.3 collective-permute-start.1
  10.8 11.8 %collective-permute-done.1 = bf16[512,384]{1,0:T(8,128)(2,1)S(1)} collective-permute-done((bf16[512,384]{1,0:T(8,128)(2,1)}, bf16[512,384]{1,0:T(8,128)(2,1)S(1)}, u32[]{:S(2)}, u32[]{:S(2)}) %collective-permute-start.1) | collective-permute-done | bytes 393248 | tf_op jit(solution)/shard_map/ppermute | solution.py:13
  22.6 0.7 copy-done.8
  23.4 0.0 all-gather.7.cloned.1.call-start
  23.4 3.8 collective-permute-start
  27.3 8.0 %collective-permute-done = bf16[512,384]{1,0:T(8,128)(2,1)S(1)} collective-permute-done((bf16[512,384]{1,0:T(8,128)(2,1)}, bf16[512,384]{1,0:T(8,128)(2,1)S(1)}, u32[]{:S(2)}, u32[]{:S(2)}) %collective-permute-start) | collective-permute-done | bytes 393248 | tf_op jit(solution)/shard_map/ppermute | solution.py:13
  35.3 0.7 copy-done.9
  36.0 0.0 all-gather.13.cloned.1.call-start
  36.1 5.5 %all-gather.9.cloned.1.call-done = bf16[512,1536]{1,0:T(8,128)(2,1)} async-done(((bf16[512,384]{1,0:T(8,128)(2,1)}), bf16[512,1536]{1,0:T(8,128)(2,1)}) %all-gather.9.cloned.1.call-update) | async-done | bytes 1572880 | tf_op jit(solution)/shard_map/all_gather | solution.py:49
  41.5 3.6 fusion.10
  45.2 27.9 %all-gather.11.cloned.1.call-done = bf16[512,1536]{1,0:T(8,128)(2,1)} async-done(((bf16[512,384]{1,0:T(8,128)(2,1)}), bf16[512,1536]{1,0:T(8,128)(2,1)}) %all-gather.11.cloned.1.call-update) | async-done | bytes 1572880 | tf_op jit(solution)/shard_map/all_gather | solution.py:51
  73.1 3.6 fusion.6
  76.7 27.4 %all-gather.7.cloned.1.call-done = bf16[512,1536]{1,0:T(8,128)(2,1)} async-done(((bf16[512,384]{1,0:T(8,128)(2,1)}), bf16[512,1536]{1,0:T(8,128)(2,1)}) %all-gather.7.cloned.1.call-update) | async-done | bytes 1572880 | tf_op jit(solution)/shard_map/all_gather | solution.py:50
  104.1 3.9 fusion.3
  108.1 0.0 reduce-scatter.4.cloned.1.call-start
  108.1 29.2 %all-gather.13.cloned.1.call-done = bf16[512,1536]{1,0:T(8,128)(2,1)} async-done(((bf16[512,384]{1,0:T(8,128)(2,1)}), bf16[512,1536]{1,0:T(8,128)(2,1)}) %all-gather.13.cloned.1.call-update) | async-done | bytes 1572880 | tf_op jit(solution)/shard_map/all_gather | solution.py:59
  137.4 5.8 %convert_reduce_fusion = (f32[4,1024]{1,0:T(4,128)}, bf16[512,1024]{1,0:T(8,128)(2,1)}, f32[512,1024]{1,0:T(8,128)S(1)}) fusion(bf16[512,1536]{1,0:T(8,128)(2,1)} %all-gather.13.cloned.1.call-done, bf16[1536,1024]{1,0:T(8,128)(2,1)S(1)} %copy-done), kind=kOutput, calls=%fused_computation.8 | convolution fusion | flops 1615327232 | bytes 7880704 | tf_op jit(solution)/shard_map/dot_general | solution.py:60
  143.2 3.5 fusion.15
  146.7 0.0 all-gather.15.cloned.1.call-start
  146.8 0.5 all-gather.15.cloned.1.call-update
  147.3 0.0 reduce-scatter.6.cloned.1.call-start
  147.3 40.1 %reduce-scatter.4.cloned.1.call-done = f32[512,384]{1,0:T(8,128)} async-done(((f32[512,1536]{1,0:T(8,128)}), f32[512,384]{1,0:T(8,128)}) %reduce-scatter.4.cloned.1.call-update) | async-done | bytes 786448 | tf_op jit(solution)/shard_map/reduce_scatter | solution.py:63
  187.4 1.2 convert_element_type.37
  188.6 3.7 collective-permute-start.3
  192.4 1.3 collective-permute-start.2
  193.7 2.3 fusion.8
  196.0 4.8 %collective-permute-done.3 = bf16[512,384]{1,0:T(8,128)(2,1)S(1)} collective-permute-done((bf16[512,384]{1,0:T(8,128)(2,1)S(1)}, bf16[512,384]{1,0:T(8,128)(2,1)S(1)}, u32[]{:S(2)}, u32[]{:S(2)}) %collective-permute-start.3) | collective-permute-done | bytes 393248 | tf_op jit(solution)/shard_map/ppermute | solution.py:13
  200.8 1.0 fusion.4
  201.8 3.1 collective-permute-done.2
  204.9 0.7 copy-done.4
  205.6 2.7 fusion
  208.4 0.2 reduce-scatter.8.cloned.1.call-start
  208.6 2.6 convolution_bitcast_fusion.1
  211.3 1.0 convolution_bitcast_fusion
  212.3 1.0 convolution_bitcast_fusion.2
  213.3 3.3 pad_maximum_fusion
  216.7 0.7 copy-done.10
  217.4 0.1 convert_reduce_fusion.1
  217.4 50.6 %all-gather.15.cloned.1.call-done = f32[64,4,1024]{2,1,0:T(4,128)} async-done(((f32[1,4,1024]{2,1,0:T(4,128)}), f32[64,4,1024]{2,1,0:T(4,128)}) %all-gather.15.cloned.1.call-update) | async-done | bytes 1048592 | tf_op jit(solution)/shard_map/all_gather | solution.py:87
  268.0 2.6 reshape.20
  270.6 2.4 convolution_multiply_fusion
  273.1 34.8 %reduce-scatter.6.cloned.1.call-done = f32[512,384]{1,0:T(8,128)} async-done(((f32[512,1536]{1,0:T(8,128)}), f32[512,384]{1,0:T(8,128)}) %reduce-scatter.6.cloned.1.call-update) | async-done | bytes 786448 | tf_op jit(solution)/shard_map/reduce_scatter | solution.py:75
  307.9 2.7 fusion.26
  310.6 151.5 %reduce-scatter.8.cloned.1.call-done = f32[3,24,384]{2,1,0:T(8,128)} async-done(((f32[3,1536,384]{2,1,0:T(8,128)}), f32[3,24,384]{2,1,0:T(8,128)}) %reduce-scatter.8.cloned.1.call-update) | async-done | bytes 110608 | tf_op jit(solution)/shard_map/reduce_scatter | solution.py:79
  (28 shorter events, 0.2 us)
Async XLA Ops:
  7.2 130.2 %copy-start = (bf16[1536,1024]{1,0:T(8,128)(2,1)S(1)}, bf16[1536,1024]{1,0:T(8,128)(2,1)}, u32[]{:S(2)}) copy-start(bf16[1536,1024]{1,0:T(8,128)(2,1)} %param.7) | copy-start | bytes 9437188
  7.2 34.4 %all-gather.9.cloned.1.call-start = ((), (), s32[]{:S(2)}) async-start(), calls=%async_computation.4 | async-start | bytes 1966080 | tf_op jit(solution)/shard_map/all_gather | solution.py:49
  9.4 63.7 %all-gather.11.cloned.1.call-start = ((), (), s32[]{:S(2)}) async-start(), calls=%async_computation.5 | async-start | bytes 1966080 | tf_op jit(solution)/shard_map/all_gather | solution.py:51
  9.5 13.1 %collective-permute-start.1 = (bf16[512,384]{1,0:T(8,128)(2,1)}, bf16[512,384]{1,0:T(8,128)(2,1)S(1)}, u32[]{:S(2)}, u32[]{:S(2)}) collective-permute-start(bf16[512,384]{1,0:T(8,128)(2,1)} %fusion.30), channel_id=1, source_target_pairs={{8,0},{12,4},{16,8},{20,12},{24,16},{28,20},{32,24},{36,28},{40,32... | collective-permute-start | bytes 1179656 | tf_op jit(solution)/shard_map/ppermute | solution.py:13
  22.6 0.7 copy-start.8
  23.4 80.7 %all-gather.7.cloned.1.call-start = ((), (), s32[]{:S(2)}) async-start(), calls=%async_computation.3 | async-start | bytes 1966080 | tf_op jit(solution)/shard_map/all_gather | solution.py:50
  23.4 11.8 %collective-permute-start = (bf16[512,384]{1,0:T(8,128)(2,1)}, bf16[512,384]{1,0:T(8,128)(2,1)S(1)}, u32[]{:S(2)}, u32[]{:S(2)}) collective-permute-start(bf16[512,384]{1,0:T(8,128)(2,1)} %fusion.30), channel_id=1, source_target_pairs={{0,8},{4,12},{8,16},{12,20},{16,24},{20,28},{24,32},{28,36},{32,40... | collective-permute-start | bytes 1179656 | tf_op jit(solution)/shard_map/ppermute | solution.py:13
  35.3 0.7 copy-start.9
  36.0 101.3 %all-gather.13.cloned.1.call-start = ((), (), s32[]{:S(2)}) async-start(), calls=%async_computation.6 | async-start | bytes 1966080 | tf_op jit(solution)/shard_map/all_gather | solution.py:59
  45.2 59.0 %copy-start.2 = (bf16[512,384]{1,0:T(8,128)(2,1)S(1)}, bf16[512,384]{1,0:T(8,128)(2,1)}, u32[]{:S(2)}) copy-start(bf16[512,384]{1,0:T(8,128)(2,1)} %param.5) | copy-start | bytes 1179652
  108.1 79.3 %reduce-scatter.4.cloned.1.call-start = ((), (), s32[]{:S(2)}) async-start(), calls=%async_computation.7 | async-start | bytes 3932160 | tf_op jit(solution)/shard_map/reduce_scatter | solution.py:63
  137.4 5.8 %copy-start.12 = (bf16[512,1024]{1,0:T(8,128)(2,1)S(1)}, bf16[512,1024]{1,0:T(8,128)(2,1)}, u32[]{:S(2)}) copy-start(bf16[512,1024]{1,0:T(8,128)(2,1)} %param.8) | copy-start | bytes 3145732
  146.7 121.3 %all-gather.15.cloned.1.call-start = ((), (), s32[]{:S(2)}) async-start(), calls=%async_computation.10 | async-start | bytes 1064960 | tf_op jit(solution)/shard_map/all_gather | solution.py:87
  147.3 160.6 %reduce-scatter.6.cloned.1.call-start = ((), (), s32[]{:S(2)}) async-start(), calls=%async_computation.8 | async-start | bytes 3932160 | tf_op jit(solution)/shard_map/reduce_scatter | solution.py:75
  188.6 7.4 %copy-start.3 = (bf16[512,384]{1,0:T(8,128)(2,1)}, bf16[512,384]{1,0:T(8,128)(2,1)S(1)}, u32[]{:S(2)}) copy-start(bf16[512,384]{1,0:T(8,128)(2,1)S(1)} %convert_element_type.37) | copy-start | bytes 1179652
  188.6 12.1 %copy-start.1 = (bf16[1,3,1536,384]{3,2,1,0:T(8,128)(2,1)S(1)}, bf16[1,3,1536,384]{3,2,1,0:T(8,128)(2,1)}, u32[]{:S(2)}) copy-start(bf16[1,3,1536,384]{3,2,1,0:T(8,128)(2,1)} %param.6) | copy-start | bytes 10616836
  188.6 12.1 %collective-permute-start.3 = (bf16[512,384]{1,0:T(8,128)(2,1)S(1)}, bf16[512,384]{1,0:T(8,128)(2,1)S(1)}, u32[]{:S(2)}, u32[]{:S(2)}) collective-permute-start(bf16[512,384]{1,0:T(8,128)(2,1)S(1)} %convert_element_type.37), channel_id=1, source_target_pairs={{0,8},{4,12},{8,16},{12,20},{16,24},{20,28},{24,32},{28,36},{32,40... | collective-permute-start | bytes 1179656 | tf_op jit(solution)/shard_map/ppermute | solution.py:13
  192.4 12.5 %collective-permute-start.2 = (bf16[512,384]{1,0:T(8,128)(2,1)S(1)}, bf16[512,384]{1,0:T(8,128)(2,1)S(1)}, u32[]{:S(2)}, u32[]{:S(2)}) collective-permute-start(bf16[512,384]{1,0:T(8,128)(2,1)S(1)} %convert_element_type.37), channel_id=1, source_target_pairs={{8,0},{12,4},{16,8},{20,12},{24,16},{28,20},{32,24},{36,28},{40,32... | collective-permute-start | bytes 1179656 | tf_op jit(solution)/shard_map/ppermute | solution.py:13
  200.8 1.0 copy-start.6
  204.9 0.7 copy-start.4
  208.4 253.7 %reduce-scatter.8.cloned.1.call-start = ((), (), s32[]{:S(2)}) async-start(), calls=%async_computation.9 | async-start | bytes 7188480 | tf_op jit(solution)/shard_map/reduce_scatter | solution.py:79
  208.6 2.7 copy-start.7
  208.6 2.6 copy-start.11
  211.3 1.0 copy-start.5
  216.7 0.7 copy-start.10
Sparse Core Ops, SparseCore 0:
  10.4 31.0 all-gather.8
  44.0 29.1 all-gather.10
  75.0 29.1 all-gather.6
  108.2 29.1 all-gather.12
  146.8 40.5 reduce-scatter.3
  190.6 77.3 all-gather.14
  270.6 37.2 reduce-scatter.5
  312.7 149.2 reduce-scatter.7
where the time goes:
time: 469 us
  waiting for transfers between devices  395 us (84%)
  matrix products  33.6 us (7%)
  between operations  14.3 us (3%)
  starting transfers between devices  10.7 us (2%)
  other arithmetic  9.47 us (2%)
  local copies, waits for them, and re-layouts  5.52 us (1%)
    reduce_scatter x1, waiting for transfers between devices, shards(): lax.psum_scatter(kernel, 'seq', scatter_dimension=1, tiled=True)  151 us
    all_gather x1, waiting for transfers between devices, shards(): all_blocks = lax.all_gather(block_partial_sums, 'seq', axis=0, tiled=True)  50.6 us
    reduce_scatter x1, waiting for transfers between devices, shards(): lax.psum_scatter(times_t(head_term, head_weight), 'chan', scatter_dimensi...  40.1 us
    reduce_scatter x1, waiting for transfers between devices, shards(): lax.psum_scatter(partial_value, 'chan', scatter_dimension=1, tiled=True)  34.8 us
    all_gather x1, waiting for transfers between devices, shards(): full_state = lax.all_gather(state, 'chan', axis=1, tiled=True)  29.2 us
    all_gather x1, waiting for transfers between devices, shards(): whole_up = lax.all_gather(upper, 'chan', axis=1, tiled=True)  27.9 us
    ppermute x4, waiting for transfers between devices, shifted(): lax.ppermute(value, axis, [(source, source + steps) for source in range(l...  27.7 us
    all_gather x1, waiting for transfers between devices, shards(): whole_low = lax.all_gather(lower, 'chan', axis=1, tiled=True)  27.4 us
  transfers between devices with their start and end apart: 12, of which 12 were waited for; matrix products, arithmetic and copies ran while one was open for 6% of the time, Pallas kernels for 0%

commit v1 on v0

--- a/solution.py
+++ b/solution.py
@@ -1,3 +1,4 @@
+import functools
 import jax
 import jax.numpy as jnp
 from jax import lax
@@ -5,6 +6,17 @@
 
 BLOCK = 128
 EXONS = 8
+
+
+def panels_match(chunk, d_out):
+    n_all = jax.lax.psum(1, "chan")
+    sides = list(map(lambda k0: n_all if k0 == d_out else 1, range(chunk.ndim)))
+    return jax.lax.all_to_all(
+        jnp.tile(chunk, sides), "chan", split_axis=d_out, concat_axis=d_out, tiled=True
+    )
+
+
+switch_marks = functools.partial(panels_match, d_out=1)
 
 
 def shifted(value, axis, steps):
@@ -56,7 +68,7 @@
     )
     saved = [(state, whole, steps)]
     state = (state.astype(jnp.float32) + mixed).astype(jnp.bfloat16)
-    full_state = lax.all_gather(state, "chan", axis=1, tiled=True)
+    full_state = switch_marks(state)
     logits = jnp.dot(full_state, head_weight, preferred_element_type=jnp.float32)
     tracks = jax.nn.softplus(logits).astype(jnp.bfloat16)
     head_term = (head_cot.astype(jnp.float32) * jax.nn.sigmoid(logits)).astype(jnp.bfloat16)

time: 469 us -> 465 us (level)
  waiting for transfers between devices: 395 us -> 365 us
  blocking collectives: 0 us -> 24.2 us
    all_gather x1 -> x0, waiting for transfers between devices: 29.2 us -> none  [shards(): full_state = lax.all_gather(state, 'chan', axis=1, tiled=True)]
    all_to_all x0 -> x1, blocking collectives: none -> 24.2 us  [panels_match(): jax.lax.all_to_all(jnp.tile(chunk, sides), 'chan', split_axis=d_out, conc...]
  transfers between devices with their start and end apart: 12 -> 11, of which waited for: 12 -> 11; matrix products, arithmetic and copies ran while one was open for 6% -> 6% of each run, Pallas kernels for 0% -> 0%
where the time goes in v1:
time: 465 us
  waiting for transfers between devices  365 us (78%)
  matrix products  32.8 us (7%)
  blocking collectives  24.2 us (5%)
  between operations  14.3 us (3%)
  starting transfers between devices  10.6 us (2%)
  other arithmetic  9.47 us (2%)
  local copies, waits for them, and re-layouts  8.27 us (2%)
    reduce_scatter x1, waiting for transfers between devices, shards(): lax.psum_scatter(kernel, 'seq', scatter_dimension=1, tiled=True)  151 us
    all_gather x1, waiting for transfers between devices, shards(): all_blocks = lax.all_gather(block_partial_sums, 'seq', axis=0, tiled=True)  50.6 us
    reduce_scatter x1, waiting for transfers between devices, shards(): lax.psum_scatter(times_t(head_term, head_weight), 'chan', scatter_dimensi...  39.4 us
    reduce_scatter x1, waiting for transfers between devices, shards(): lax.psum_scatter(partial_value, 'chan', scatter_dimension=1, tiled=True)  34.7 us
    all_gather x1, waiting for transfers between devices, shards(): whole_up = lax.all_gather(upper, 'chan', axis=1, tiled=True)  27.9 us
    ppermute x4, waiting for transfers between devices, shifted(): lax.ppermute(value, axis, [(source, source + steps) for source in range(l...  27.7 us
    all_gather x1, waiting for transfers between devices, shards(): whole_low = lax.all_gather(lower, 'chan', axis=1, tiled=True)  27.4 us
    all_to_all x1, blocking collectives, panels_match(): jax.lax.all_to_all(jnp.tile(chunk, sides), 'chan', split_axis=d_out, conc...  24.2 us
  transfers between devices with their start and end apart: 11, of which 11 were waited for; matrix products, arithmetic and copies ran while one was open for 6% of the time, Pallas kernels for 0%

profile of v1, /device:TPU:2, one launch (start us, length us, event | category | flops | bytes accessed | tf_op | source)
XLA Modules:
  0.0 464.9 jit_solution(10573736296879879602)
XLA Ops:
  7.2 0.0 all-gather.8.cloned.1.call-start
  7.2 2.2 fusion.30
  9.4 0.0 all-gather.10.cloned.1.call-start
  9.5 1.3 collective-permute-start.1
  10.8 11.8 %collective-permute-done.1 = bf16[512,384]{1,0:T(8,128)(2,1)S(1)} collective-permute-done((bf16[512,384]{1,0:T(8,128)(2,1)}, bf16[512,384]{1,0:T(8,128)(2,1)S(1)}, u32[]{:S(2)}, u32[]{:S(2)}) %collective-permute-start.1) | collective-permute-done | bytes 393248 | tf_op jit(solution)/shard_map/ppermute | solution.py:25
  22.6 0.7 copy-done.8
  23.4 0.0 all-gather.6.cloned.1.call-start
  23.4 3.8 collective-permute-start
  27.3 8.0 %collective-permute-done = bf16[512,384]{1,0:T(8,128)(2,1)S(1)} collective-permute-done((bf16[512,384]{1,0:T(8,128)(2,1)}, bf16[512,384]{1,0:T(8,128)(2,1)S(1)}, u32[]{:S(2)}, u32[]{:S(2)}) %collective-permute-start) | collective-permute-done | bytes 393248 | tf_op jit(solution)/shard_map/ppermute | solution.py:25
  35.3 0.8 copy-done.9
  36.1 0.0 reduce-scatter.4.cloned.1.call-start
  36.1 5.4 %all-gather.8.cloned.1.call-done = bf16[512,1536]{1,0:T(8,128)(2,1)} async-done(((bf16[512,384]{1,0:T(8,128)(2,1)}), bf16[512,1536]{1,0:T(8,128)(2,1)}) %all-gather.8.cloned.1.call-update) | async-done | bytes 1572880 | tf_op jit(solution)/shard_map/all_gather | solution.py:61
  41.5 3.6 fusion.10
  45.2 27.9 %all-gather.10.cloned.1.call-done = bf16[512,1536]{1,0:T(8,128)(2,1)} async-done(((bf16[512,384]{1,0:T(8,128)(2,1)}), bf16[512,1536]{1,0:T(8,128)(2,1)}) %all-gather.10.cloned.1.call-update) | async-done | bytes 1572880 | tf_op jit(solution)/shard_map/all_gather | solution.py:63
  73.1 3.6 fusion.6
  76.7 27.4 %all-gather.6.cloned.1.call-done = bf16[512,1536]{1,0:T(8,128)(2,1)} async-done(((bf16[512,384]{1,0:T(8,128)(2,1)}), bf16[512,1536]{1,0:T(8,128)(2,1)}) %all-gather.6.cloned.1.call-update) | async-done | bytes 1572880 | tf_op jit(solution)/shard_map/all_gather | solution.py:62
  104.1 3.2 fusion.3
  107.3 0.1 tile.2
  107.5 24.2 %all_to_all.9 = bf16[512,4,384]{2,0,1:T(8,128)(2,1)} all-to-all(bf16[512,4,384]{2,0,1:T(8,128)(2,1)S(1)} %tile.2), channel_id=1, replica_groups=mesh['seq'=64,'chan'=4] {'chan'}, dimensions={1} | all-to-all | bytes 3145728 | tf_op jit(solution)/shard_map/all_to_all | solution.py:14
  131.7 2.6 copy.10
  134.3 5.9 %convert_reduce_fusion = (f32[4,1024]{1,0:T(4,128)}, bf16[512,1024]{1,0:T(8,128)(2,1)}, f32[512,1024]{1,0:T(8,128)S(1)}) fusion(bf16[512,1536]{0,1:T(8,128)(2,1)} %bitcast.44, bf16[1536,1024]{1,0:T(8,128)(2,1)S(1)} %copy-done), kind=kOutput, calls=%fused_computation.8 | convolution fusion | flops 1615327232 | bytes 7880704 | tf_op jit(solution)/shard_map/dot_general | solution.py:72
  140.1 3.5 fusion.15
  143.6 0.0 all-gather.12.cloned.1.call-start
  143.7 0.5 all-gather.12.cloned.1.call-update
  144.2 0.0 reduce-scatter.6.cloned.1.call-start
  144.3 39.4 %reduce-scatter.4.cloned.1.call-done = f32[512,384]{1,0:T(8,128)} async-done(((f32[512,1536]{1,0:T(8,128)}), f32[512,384]{1,0:T(8,128)}) %reduce-scatter.4.cloned.1.call-update) | async-done | bytes 786448 | tf_op jit(solution)/shard_map/reduce_scatter | solution.py:75
  183.7 1.2 convert_element_type.37
  184.9 3.8 collective-permute-start.3
  188.7 1.3 collective-permute-start.2
  190.0 2.3 fusion.8
  192.3 4.8 %collective-permute-done.3 = bf16[512,384]{1,0:T(8,128)(2,1)S(1)} collective-permute-done((bf16[512,384]{1,0:T(8,128)(2,1)S(1)}, bf16[512,384]{1,0:T(8,128)(2,1)S(1)}, u32[]{:S(2)}, u32[]{:S(2)}) %collective-permute-start.3) | collective-permute-done | bytes 393248 | tf_op jit(solution)/shard_map/ppermute | solution.py:25
  197.0 1.0 fusion.4
  198.1 3.1 collective-permute-done.2
  201.2 0.7 copy-done.4
  201.9 2.7 fusion
  204.7 0.2 reduce-scatter.8.cloned.1.call-start
  204.9 2.6 convolution_bitcast_fusion.1
  207.6 1.0 convolution_bitcast_fusion
  208.6 1.0 convolution_bitcast_fusion.2
  209.6 3.3 pad_maximum_fusion
  213.0 0.7 copy-done.10
  213.6 0.1 convert_reduce_fusion.1
  213.7 50.6 %all-gather.12.cloned.1.call-done = f32[64,4,1024]{2,1,0:T(4,128)} async-done(((f32[1,4,1024]{2,1,0:T(4,128)}), f32[64,4,1024]{2,1,0:T(4,128)}) %all-gather.12.cloned.1.call-update) | async-done | bytes 1048592 | tf_op jit(solution)/shard_map/all_gather | solution.py:99
  264.3 2.6 reshape.27
  266.9 2.4 convolution_multiply_fusion
  269.3 34.7 %reduce-scatter.6.cloned.1.call-done = f32[512,384]{1,0:T(8,128)} async-done(((f32[512,1536]{1,0:T(8,128)}), f32[512,384]{1,0:T(8,128)}) %reduce-scatter.6.cloned.1.call-update) | async-done | bytes 786448 | tf_op jit(solution)/shard_map/reduce_scatter | solution.py:87
  304.0 2.7 fusion.26
  306.7 151.3 %reduce-scatter.8.cloned.1.call-done = f32[3,24,384]{2,1,0:T(8,128)} async-done(((f32[3,1536,384]{2,1,0:T(8,128)}), f32[3,24,384]{2,1,0:T(8,128)}) %reduce-scatter.8.cloned.1.call-update) | async-done | bytes 110608 | tf_op jit(solution)/shard_map/reduce_scatter | solution.py:91
  (28 shorter events, 0.2 us)
Async XLA Ops:
  7.2 127.1 %copy-start = (bf16[1536,1024]{1,0:T(8,128)(2,1)S(1)}, bf16[1536,1024]{1,0:T(8,128)(2,1)}, u32[]{:S(2)}) copy-start(bf16[1536,1024]{1,0:T(8,128)(2,1)} %param.7) | copy-start | bytes 9437188
  7.2 34.4 %all-gather.8.cloned.1.call-start = ((), (), s32[]{:S(2)}) async-start(), calls=%async_computation.5 | async-start | bytes 1966080 | tf_op jit(solution)/shard_map/all_gather | solution.py:61
  9.4 63.7 %all-gather.10.cloned.1.call-start = ((), (), s32[]{:S(2)}) async-start(), calls=%async_computation.6 | async-start | bytes 1966080 | tf_op jit(solution)/shard_map/all_gather | solution.py:63
  9.5 13.1 %collective-permute-start.1 = (bf16[512,384]{1,0:T(8,128)(2,1)}, bf16[512,384]{1,0:T(8,128)(2,1)S(1)}, u32[]{:S(2)}, u32[]{:S(2)}) collective-permute-start(bf16[512,384]{1,0:T(8,128)(2,1)} %fusion.30), channel_id=1, source_target_pairs={{8,0},{12,4},{16,8},{20,12},{24,16},{28,20},{32,24},{36,28},{40,32... | collective-permute-start | bytes 1179656 | tf_op jit(solution)/shard_map/ppermute | solution.py:25
  22.6 0.7 copy-start.8
  23.4 80.7 %all-gather.6.cloned.1.call-start = ((), (), s32[]{:S(2)}) async-start(), calls=%async_computation.4 | async-start | bytes 1966080 | tf_op jit(solution)/shard_map/all_gather | solution.py:62
  23.4 11.8 %collective-permute-start = (bf16[512,384]{1,0:T(8,128)(2,1)}, bf16[512,384]{1,0:T(8,128)(2,1)S(1)}, u32[]{:S(2)}, u32[]{:S(2)}) collective-permute-start(bf16[512,384]{1,0:T(8,128)(2,1)} %fusion.30), channel_id=1, source_target_pairs={{0,8},{4,12},{8,16},{12,20},{16,24},{20,28},{24,32},{28,36},{32,40... | collective-permute-start | bytes 1179656 | tf_op jit(solution)/shard_map/ppermute | solution.py:25
  35.3 0.8 copy-start.9
  36.1 147.6 %reduce-scatter.4.cloned.1.call-start = ((), (), s32[]{:S(2)}) async-start(), calls=%async_computation.7 | async-start | bytes 3932160 | tf_op jit(solution)/shard_map/reduce_scatter | solution.py:75
  45.2 59.0 %copy-start.2 = (bf16[512,384]{1,0:T(8,128)(2,1)S(1)}, bf16[512,384]{1,0:T(8,128)(2,1)}, u32[]{:S(2)}) copy-start(bf16[512,384]{1,0:T(8,128)(2,1)} %param.5) | copy-start | bytes 1179652
  134.3 5.9 %copy-start.12 = (bf16[512,1024]{1,0:T(8,128)(2,1)S(1)}, bf16[512,1024]{1,0:T(8,128)(2,1)}, u32[]{:S(2)}) copy-start(bf16[512,1024]{1,0:T(8,128)(2,1)} %param.8) | copy-start | bytes 3145732
  143.6 120.7 %all-gather.12.cloned.1.call-start = ((), (), s32[]{:S(2)}) async-start(), calls=%async_computation.10 | async-start | bytes 1064960 | tf_op jit(solution)/shard_map/all_gather | solution.py:99
  144.2 159.8 %reduce-scatter.6.cloned.1.call-start = ((), (), s32[]{:S(2)}) async-start(), calls=%async_computation.8 | async-start | bytes 3932160 | tf_op jit(solution)/shard_map/reduce_scatter | solution.py:87
  184.9 7.4 %copy-start.3 = (bf16[512,384]{1,0:T(8,128)(2,1)}, bf16[512,384]{1,0:T(8,128)(2,1)S(1)}, u32[]{:S(2)}) copy-start(bf16[512,384]{1,0:T(8,128)(2,1)S(1)} %convert_element_type.37) | copy-start | bytes 1179652
  184.9 12.2 %copy-start.1 = (bf16[1,3,1536,384]{3,2,1,0:T(8,128)(2,1)S(1)}, bf16[1,3,1536,384]{3,2,1,0:T(8,128)(2,1)}, u32[]{:S(2)}) copy-start(bf16[1,3,1536,384]{3,2,1,0:T(8,128)(2,1)} %param.6) | copy-start | bytes 10616836
  184.9 12.1 %collective-permute-start.3 = (bf16[512,384]{1,0:T(8,128)(2,1)S(1)}, bf16[512,384]{1,0:T(8,128)(2,1)S(1)}, u32[]{:S(2)}, u32[]{:S(2)}) collective-permute-start(bf16[512,384]{1,0:T(8,128)(2,1)S(1)} %convert_element_type.37), channel_id=1, source_target_pairs={{0,8},{4,12},{8,16},{12,20},{16,24},{20,28},{24,32},{28,36},{32,40... | collective-permute-start | bytes 1179656 | tf_op jit(solution)/shard_map/ppermute | solution.py:25
  188.7 12.5 %collective-permute-start.2 = (bf16[512,384]{1,0:T(8,128)(2,1)S(1)}, bf16[512,384]{1,0:T(8,128)(2,1)S(1)}, u32[]{:S(2)}, u32[]{:S(2)}) collective-permute-start(bf16[512,384]{1,0:T(8,128)(2,1)S(1)} %convert_element_type.37), channel_id=1, source_target_pairs={{8,0},{12,4},{16,8},{20,12},{24,16},{28,20},{32,24},{36,28},{40,32... | collective-permute-start | bytes 1179656 | tf_op jit(solution)/shard_map/ppermute | solution.py:25
  197.0 1.0 copy-start.6
  201.2 0.7 copy-start.4
  204.7 253.3 %reduce-scatter.8.cloned.1.call-start = ((), (), s32[]{:S(2)}) async-start(), calls=%async_computation.9 | async-start | bytes 7188480 | tf_op jit(solution)/shard_map/reduce_scatter | solution.py:91
  204.9 2.7 copy-start.7
  204.9 2.6 copy-start.11
  207.6 1.0 copy-start.5
  212.9 0.7 copy-start.10
Sparse Core Ops, SparseCore 0:
  10.4 31.0 all-gather.7
  44.0 29.1 all-gather.9
  75.0 29.1 all-gather.5
  143.7 39.9 reduce-scatter.3
  186.9 77.3 all-gather.11
  266.7 37.2 reduce-scatter.5
  308.9 149.1 reduce-scatter.7
